TPU v7x, 32 devices: a whole 2x2x4 slice. The times are simulated.
32 devices in a mesh: expert: 4 (over z), mp: 8 (over y, x, core).
Axes of the slice: x: 2, y: 2, z: 4, core: 2. Of those that a mesh axis runs over, the one named last changes fastest.
Arguments:
- x_tokens: bfloat16 [512, 2048], P('expert', 'mp'), may hold values from -6 to 6
- cotangent: bfloat16 [512, 2048], P('expert', 'mp'), may hold values from -2 to 2
- w_gate: bfloat16 [4, 1024, 8192], P('expert', None, 'mp'), may hold values from -0.125 to 0.125
- w_up: bfloat16 [4, 1024, 8192], P('expert', None, 'mp'), may hold values from -0.125 to 0.125
- w_down: bfloat16 [4, 8192, 1024], P('expert', 'mp'), may hold values from -0.125 to 0.125
- combine: float32 [8, 128], P('expert'), may hold values from 0.1 to 1
- indices: int32 [8, 128], replicated, may hold values from -1 to 511, as said below
Outputs:
- grad_tokens: bfloat16 [512, 2048], P('expert', 'mp')
- grad_gate: bfloat16 [4, 1024, 8192], P('expert', None, 'mp')
- grad_up: bfloat16 [4, 1024, 8192], P('expert', None, 'mp')
- grad_down: bfloat16 [4, 8192, 1024], P('expert', 'mp')
- grad_combine: float32 [8, 128], P('expert')
Inputs may be any that keep to these rules, and one draw needn't show every extreme that they name: `indices`: each row lists the tokens one expert chose, in increasing order, then -1 in its remaining slots. Tokens are owned in blocks of 128 along expert; one expert takes at most 64 tokens from one block, and in every row some block gives exactly 64. In every draw some expert fills all 128 slots.
All inputs are finite; a program needn't handle non-finite values.
Results may differ from a plain program's by a relative error of at most 0.022.
Values may be sent and summed in bfloat16 or wider, within the bound.
A program may use at most 64 MiB of HBM per device.

v0:
```python
import jax
import jax.numpy as jnp
from jax import lax
from jax.sharding import PartitionSpec as P


def from_partner(block, axis, distance):
    count = lax.axis_size(axis)
    route = []
    for low in range(count):
        high = low | 1 << distance
        if high != low and high < count:
            route += [(low, high), (high, low)]
    return lax.ppermute(block, axis, route)


def local(x_tokens, cotangent, w_gate, w_up, w_down, combine, indices):
    groups = lax.axis_size("expert")
    lane_count = lax.axis_size("mp")
    tok_dev, width_part = x_tokens.shape
    experts, capacity = indices.shape
    exp_dev = experts // groups
    peer_slots = 2 * capacity // groups
    half_width = w_gate.shape[1]
    hidden = w_gate.shape[2]
    per_expert = lane_count // exp_dev
    blocks = per_expert // 2
    half_lanes = lane_count // 2
    group_index = lax.axis_index("expert")
    lane_index = lax.axis_index("mp")
    own_expert = lane_index // per_expert
    own_half = lane_index // blocks % 2
    offsets = jnp.arange(peer_slots, dtype=jnp.int32)
    slot_valid = indices >= 0
    keyed = jnp.where(slot_valid, indices, groups * tok_dev)
    bounds = jnp.arange(groups + 1, dtype=jnp.int32) * tok_dev
    edges = jax.vmap(lambda row_keys: jnp.searchsorted(row_keys, bounds, side="left"))(keyed)
    slot_starts = edges[:, :-1]
    per_source = edges[:, 1:] - edges[:, :-1]
    send_start = lax.dynamic_index_in_dim(slot_starts, group_index, 1, keepdims=False)
    send_count = lax.dynamic_index_in_dim(per_source, group_index, 1, keepdims=False)
    send_live = offsets[None, :] < send_count[:, None]
    send_slot = jnp.where(send_live, send_start[:, None] + offsets[None, :], 0)
    chosen = jnp.take_along_axis(indices, send_slot, axis=1)
    local_row = jnp.where(send_live, chosen - group_index * tok_dev, 0)
    send_mask = send_live[:, :, None]
    zero_half = jnp.zeros((), jnp.bfloat16)
    send_in = jnp.where(send_mask, x_tokens[local_row], zero_half).reshape(
        groups, exp_dev, peer_slots, width_part
    )
    send_out = jnp.where(send_mask, cotangent[local_row], zero_half).reshape(
        groups, exp_dev, peer_slots, width_part
    )
    recv_in, recv_out = (
        lax.all_to_all(send_in, "expert", split_axis=0, concat_axis=0, tiled=True),
        lax.all_to_all(send_out, "expert", split_axis=0, concat_axis=0, tiled=True),
    )
    own_rows = lax.dynamic_slice_in_dim(indices, group_index * exp_dev, exp_dev, 0)
    own_valid = own_rows >= 0
    own_source = jnp.where(own_valid, own_rows // tok_dev, 0)
    own_starts = lax.dynamic_slice_in_dim(slot_starts, group_index * exp_dev, exp_dev, 0)
    own_counts = lax.dynamic_slice_in_dim(per_source, group_index * exp_dev, exp_dev, 0)
    base_slot = jnp.take_along_axis(own_starts, own_source, axis=1)
    position = jnp.arange(capacity, dtype=jnp.int32)[None, :] - base_slot
    member_ids = jnp.arange(exp_dev, dtype=jnp.int32)
    half_ids = jnp.arange(2, dtype=jnp.int32)
    flat_index = own_source * (exp_dev * peer_slots) + member_ids[:, None] * peer_slots + position
    flat_index = jnp.where(own_valid, flat_index, 0)
    compact_in = jnp.where(
        own_valid[:, :, None], recv_in.reshape(-1, width_part)[flat_index], zero_half
    )
    compact_out = jnp.where(
        own_valid[:, :, None], recv_out.reshape(-1, width_part)[flat_index], zero_half
    )
    full_in, full_out = (
        lax.all_gather(compact_in, "mp", axis=2, tiled=True),
        lax.all_gather(compact_out, "mp", axis=2, tiled=True),
    )
    whole_in = lax.dynamic_index_in_dim(full_in, own_expert, 0, keepdims=False)
    whole_out = lax.dynamic_index_in_dim(full_out, own_expert, 0, keepdims=False)
    rows_in = lax.dynamic_slice_in_dim(whole_in, own_half * half_width, half_width, 1)
    rows_out = lax.dynamic_slice_in_dim(whole_out, own_half * half_width, half_width, 1)
    wg = w_gate[0]
    wu = w_up[0]
    wd = w_down[0]
    slot_weight = lax.dynamic_index_in_dim(combine, own_expert, 0, keepdims=False)
    gate_mine = jnp.dot(rows_in, wg, preferred_element_type=jnp.float32)
    up_mine = jnp.dot(rows_in, wu, preferred_element_type=jnp.float32)
    back_mine = lax.dot_general(
        rows_out, wd, (((1,), (1,)), ((), ())), preferred_element_type=jnp.float32
    )
    gate_other, up_other, back_other = (
        from_partner(gate_mine.astype(jnp.bfloat16), "mp", blocks.bit_length() - 1).astype(
            gate_mine.dtype
        ),
        from_partner(up_mine.astype(jnp.bfloat16), "mp", blocks.bit_length() - 1).astype(
            up_mine.dtype
        ),
        from_partner(back_mine.astype(jnp.bfloat16), "mp", blocks.bit_length() - 1).astype(
            back_mine.dtype
        ),
    )
    gate_pre = gate_mine + gate_other
    up_pre = up_mine + up_other
    back_grad = back_mine + back_other
    sigmoid_gate = jax.nn.sigmoid(gate_pre)
    activation = (gate_pre * sigmoid_gate * up_pre).astype(jnp.bfloat16)
    slot_term = jnp.sum(activation.astype(jnp.float32) * back_grad, axis=1)
    term_keep = (member_ids[:, None] == own_expert) & (own_half == 0)
    term_table = jnp.where(term_keep, slot_term[None, :], 0.0)
    grad_combine = lax.psum(term_table, "mp")
    scaled_out = (slot_weight[:, None] * rows_out.astype(jnp.float32)).astype(jnp.bfloat16)
    grad_down = lax.dot_general(
        activation, scaled_out, (((0,), (0,)), ((), ())), preferred_element_type=jnp.float32
    )
    d_act = slot_weight[:, None] * back_grad
    d_gate = (d_act * up_pre * sigmoid_gate * (1.0 + gate_pre * (1.0 - sigmoid_gate))).astype(
        jnp.bfloat16
    )
    d_up = (d_act * gate_pre * sigmoid_gate).astype(jnp.bfloat16)
    grad_gate = lax.dot_general(
        rows_in, d_gate, (((0,), (0,)), ((), ())), preferred_element_type=jnp.float32
    )
    grad_up = lax.dot_general(
        rows_in, d_up, (((0,), (0,)), ((), ())), preferred_element_type=jnp.float32
    )
    partial_value = jnp.einsum(
        "ch,ldh->lcd",
        d_gate,
        wg.reshape(half_lanes, width_part, hidden),
        preferred_element_type=jnp.float32,
    )
    partial_value = partial_value + jnp.einsum(
        "ch,ldh->lcd",
        d_up,
        wu.reshape(half_lanes, width_part, hidden),
        preferred_element_type=jnp.float32,
    )
    partial_half = partial_value.astype(jnp.bfloat16)
    keep = (member_ids[:, None] == own_expert) & (half_ids[None, :] == own_half)
    padded = jnp.where(keep[:, :, None, None, None], partial_half[None, None], zero_half)
    padded = padded.reshape(exp_dev, lane_count, capacity, width_part)
    summed = lax.psum_scatter(padded, "mp", scatter_dimension=1, tiled=True).astype(jnp.float32)[
        :, 0
    ]
    back_start = jnp.transpose(own_starts)[:, :, None] + offsets[None, None, :]
    back_live = offsets[None, None, :] < jnp.transpose(own_counts)[:, :, None]
    back_index = member_ids[None, :, None] * capacity + jnp.where(back_live, back_start, 0)
    send_back = jnp.where(
        back_live[:, :, :, None], summed.reshape(exp_dev * capacity, width_part)[back_index], 0.0
    )
    returned = lax.all_to_all(
        send_back.astype(jnp.bfloat16), "expert", split_axis=0, concat_axis=0, tiled=True
    ).astype(send_back.dtype)
    targets = jnp.where(send_live, local_row, tok_dev).reshape(-1)
    gathered = (
        jnp.zeros((tok_dev + 1, width_part), jnp.float32)
        .at[targets]
        .add(returned.reshape(-1, width_part))
    )
    grad_tokens = gathered[:tok_dev].astype(jnp.bfloat16)
    return (
        grad_tokens,
        grad_gate.astype(jnp.bfloat16)[None],
        grad_up.astype(jnp.bfloat16)[None],
        grad_down.astype(jnp.bfloat16)[None],
        grad_combine,
    )


def solution(mesh):
    placed = (
        P("expert", "mp"),
        P("expert", "mp"),
        P("expert", None, "mp"),
        P("expert", None, "mp"),
        P("expert", "mp", None),
        P("expert", None),
        P(),
    )
    return jax.shard_map(
        local,
        mesh=mesh,
        in_specs=placed,
        out_specs=(
            P("expert", "mp"),
            P("expert", None, "mp"),
            P("expert", None, "mp"),
            P("expert", "mp", None),
            P("expert", None),
        ),
        check_vma=False,
    )
```

profile of v0, /device:TPU:2, one launch (start us, length us, event | category | flops | bytes accessed | tf_op | source)
XLA Modules:
  0.0 184.0 jit_solution(14584411498375059266)
XLA Ops:
  7.2 0.8 compare_select_fusion.5
  8.0 8.0 %while.24 = (s32[]{:T(128)}, u32[8,5]{1,0:T(8,128)S(1)}, u32[8,5]{1,0:T(8,128)S(1)}, s32[8,128]{1,0:T(8,128)S(1)}, s32[]{:T(128)}, /*index=5*/s32[]{:T(128)}) while((s32[]{:T(128)}, u32[8,5]{1,0:T(8,128)S(1)}, u32[8,5]{1,0:T(8,128)S(1)}, s32[8,128]{1,0:T(8,128)S(1)}, s32[]{:T(128)}, /*index=5*/s32[]{:T(128)}) %tuple.50), condition=%wide.region_1.2_spmd.clone, body=%wide.region_0.1_spmd.clone.sunk | while | flops 928 | bytes 3401 | solution.py:37
  8.1 0.1 reshape.573
  8.1 0.8 gather_fusion
  8.9 0.1 squeeze.28
  9.1 0.8 gather_fusion
  9.9 0.1 squeeze.28
  10.1 0.8 gather_fusion
  10.9 0.1 squeeze.28
  11.1 0.8 gather_fusion
  11.9 0.1 squeeze.28
  12.1 0.8 gather_fusion
  12.9 0.1 squeeze.28
  13.2 0.8 gather_fusion
  13.9 0.1 squeeze.28
  14.2 0.8 gather_fusion
  15.2 0.8 gather_fusion
  15.9 0.1 squeeze.28
  16.1 0.2 dynamic-slice_reduce_fusion
  16.4 0.1 lt.237
  16.5 0.1 shift-left_or_fusion
  16.7 2.5 %gather_fusion.6 = s32[512]{0:T(512)S(1)} fusion(s32[8,128]{1,0:T(8,128)S(1)} %copy-done.1, s32[512]{0:T(512)S(1)} %reshape.514), kind=kCustom, calls=%fused_computation.6 | custom fusion | bytes 8192 | tf_op jit(solution)/shard_map/jit(take_along_axis)/gather | solution.py:44
  19.3 0.1 compare_select_fusion.3
  19.5 1.9 %gather_fusion.3 = bf16[512,256]{1,0:T(8,128)(2,1)S(1)} fusion(bf16[128,256]{1,0:T(8,128)(2,1)S(1)} %copy-done.2, s32[1024]{0:T(1024)S(1)} %pad_clamp_fusion.2), kind=kCustom, calls=%fused_computation.3 | custom fusion | bytes 526336 | tf_op jit(solution)/shard_map/gather | solution.py:48
  21.5 2.0 %gather_fusion.1 = bf16[512,256]{1,0:T(8,128)(2,1)S(1)} fusion(bf16[128,256]{1,0:T(8,128)(2,1)S(1)} %copy-done.3, s32[1024]{0:T(1024)S(1)} %pad_clamp_fusion.2), kind=kCustom, calls=%fused_computation.1 | custom fusion | bytes 526336 | tf_op jit(solution)/shard_map/gather | solution.py:51
  23.4 0.9 broadcast_select_fusion.2
  24.3 4.9 %all-to-all-start = ((bf16[4,2,64,256]{3,2,1,0:T(8,128)(2,1)}), bf16[4,2,64,256]{3,2,1,0:T(8,128)(2,1)S(1)}, u32[]{:S(2)}, u32[]{:S(2)}) async-start(bf16[4,2,64,256]{3,2,1,0:T(8,128)(2,1)} %get-tuple-element.107), calls=%async_computation | async-start | bytes 524288 | tf_op jit(solution)/shard_map/all_to_all | solution.py:56
  29.3 2.4 %gather_fusion.7 = s32[256]{0:T(256)S(1)} fusion(s32[2,4]{1,0:T(2,128)S(1)} %get-tuple-element.119, s32[256]{0:T(256)S(1)} %get-tuple-element.100), kind=kCustom, calls=%fused_computation.7 | custom fusion | bytes 4096 | tf_op jit(solution)/shard_map/jit(take_along_axis)/gather | solution.py:63
  31.7 6.4 %all-to-all-done = bf16[4,2,64,256]{3,2,1,0:T(8,128)(2,1)S(1)} async-done(((bf16[4,2,64,256]{3,2,1,0:T(8,128)(2,1)}), bf16[4,2,64,256]{3,2,1,0:T(8,128)(2,1)S(1)}, u32[]{:S(2)}, u32[]{:S(2)}) %all-to-all-start) | async-done | bytes 262176 | tf_op jit(solution)/shard_map/all_to_all | solution.py:56
  38.1 3.4 %all-to-all-start.1 = ((bf16[4,2,64,256]{3,2,1,0:T(8,128)(2,1)}), bf16[4,2,64,256]{3,2,1,0:T(8,128)(2,1)S(1)}, u32[]{:S(2)}, u32[]{:S(2)}) async-start(bf16[4,2,64,256]{3,2,1,0:T(8,128)(2,1)} %get-tuple-element.108), calls=%async_computation.1 | async-start | bytes 524288 | tf_op jit(solution)/shard_map/all_to_all | solution.py:55
  41.7 1.2 gather_fusion.2
  42.8 5.7 %all-to-all-done.1 = bf16[4,2,64,256]{3,2,1,0:T(8,128)(2,1)S(1)} async-done(((bf16[4,2,64,256]{3,2,1,0:T(8,128)(2,1)}), bf16[4,2,64,256]{3,2,1,0:T(8,128)(2,1)S(1)}, u32[]{:S(2)}, u32[]{:S(2)}) %all-to-all-start.1) | async-done | bytes 262176 | tf_op jit(solution)/shard_map/all_to_all | solution.py:55
  48.5 1.2 gather_fusion.4
  49.7 0.8 broadcast_select_fusion.4
  50.6 0.7 all-gather.3.cloned.1.call-update
  51.4 22.4 %all-gather.5.cloned.1.call-done = bf16[2,128,2048]{2,1,0:T(8,128)(2,1)} async-done(((bf16[2,128,256]{2,1,0:T(8,128)(2,1)}), bf16[2,128,2048]{2,1,0:T(8,128)(2,1)}) %all-gather.5.cloned.1.call-update) | async-done | bytes 1048592 | tf_op jit(solution)/shard_map/all_gather | solution.py:76
  73.8 2.3 %fusion.51 = (bf16[128,1024]{1,0:T(8,128)(2,1)}, f32[128,1024]{1,0:T(8,128)S(1)}) fusion(bf16[1,1024,1024]{2,1,0:T(8,128)(2,1)S(1)} %copy-done, bf16[2,128,2048]{2,1,0:T(8,128)(2,1)} %all-gather.5.cloned.1.call-done, s32[]{:T(128)S(6)} %select_n.282, s32[]{:T(128)S(6)} %select_n.284), kind=kOutput, calls=%fused_computation.123 | convolution fusion | flops 268566528 | bytes 3145736 | tf_op jit(solution)/shard_map/dot_general | solution.py:87
  76.1 0.6 collective-permute-start.2
  76.7 2.3 %fusion.50 = (bf16[128,1024]{1,0:T(8,128)(2,1)}, f32[128,1024]{1,0:T(8,128)}) fusion(bf16[1,1024,1024]{2,1,0:T(8,128)(2,1)S(1)} %copy-done.4, bf16[2,128,2048]{2,1,0:T(8,128)(2,1)} %all-gather.5.cloned.1.call-done, s32[]{:T(128)S(6)} %select_n.282, s32[]{:T(128)S(6)} %select_n.284), kind=kOutput, calls=%fused_computation.122 | convolution fusion | flops 268566528 | bytes 3145736 | tf_op jit(solution)/shard_map/dot_general | solution.py:88
  79.0 1.5 collective-permute-start.1
  80.5 20.8 %all-gather.3.cloned.1.call-done = bf16[2,128,2048]{2,1,0:T(8,128)(2,1)} async-done(((bf16[2,128,256]{2,1,0:T(8,128)(2,1)}), bf16[2,128,2048]{2,1,0:T(8,128)(2,1)}) %all-gather.3.cloned.1.call-update) | async-done | bytes 1048592 | tf_op jit(solution)/shard_map/all_gather | solution.py:77
  101.3 3.4 %fusion.49 = (bf16[128,1024]{1,0:T(8,128)(2,1)}, f32[128,1024]{1,0:T(8,128)}) fusion(bf16[1,1024,1024]{2,1,0:T(8,128)(2,1)} %param.13, bf16[2,128,2048]{2,1,0:T(8,128)(2,1)} %all-gather.3.cloned.1.call-done, s32[]{:T(128)S(6)} %select_n.282, s32[]{:T(128)S(6)} %select_n.284), kind=kOutput, calls=%fused_computation.121 | convolution fusion | flops 268566528 | bytes 3145736 | tf_op jit(solution)/shard_map/dot_general | solution.py:89
  104.7 0.6 collective-permute-start
  105.4 0.1 copy.21
  105.5 7.9 %collective-permute-done = bf16[128,1024]{1,0:T(8,128)(2,1)S(1)} collective-permute-done((bf16[128,1024]{1,0:T(8,128)(2,1)}, bf16[128,1024]{1,0:T(8,128)(2,1)S(1)}, u32[]{:S(2)}, u32[]{:S(2)}) %collective-permute-start) | collective-permute-done | bytes 262176 | tf_op jit(solution)/shard_map/ppermute | solution.py:14
  113.4 0.7 copy-done.8
  114.1 1.9 %multiply_reduce_fusion = (f32[128]{0:T(128)S(1)}, bf16[128,1024]{1,0:T(8,128)(2,1)S(1)}, bf16[128,1024]{1,0:T(8,128)(2,1)S(1)}, bf16[128,1024]{1,0:T(8,128)(2,1)S(1)}) fusion(f32[128,1024]{1,0:T(8,128)} %get-tuple-element.112, bf16[128,1024]{1,0:T(8,128)(2,1)} %copy-done.8, f32[128,1024]{1,0:T(8,128)} %get-tuple-element.114, ...), kind=kLoop, calls=%fused_computation.31 | loop fusion | flops 3407744 | bytes 3146752 | tf_op jit(solution)/shard_map/reduce_sum | solution.py:108
  116.0 0.8 fusion.13
  116.9 0.7 copy-done.5
  117.6 0.8 fusion.9
  118.5 1.1 broadcast_select_fusion
  119.8 0.1 copy.16
  119.9 0.1 copy.19
  120.1 0.1 reshape.508
  120.7 10.5 %psum.7 = f32[2,128]{1,0:T(2,128)} all-reduce(f32[2,128]{1,0:T(2,128)S(1)} %broadcast_select_fusion.5), channel_id=1, replica_groups=mesh['expert'=4,'mp'=8] {'mp'}, use_global_device_ids=true, to_apply=%region_5.6 | all-reduce | flops 256 | bytes 2048 | tf_op jit(solution)/shard_map/psum | solution.py:111
  131.2 24.7 %reduce-scatter.2.cloned.1.call-done = bf16[2,1,128,256]{3,2,0,1:T(8,128)(2,1)} async-done(((bf16[2,8,128,256]{3,2,0,1:T(8,128)(2,1)}), bf16[2,1,128,256]{3,2,0,1:T(8,128)(2,1)}) %reduce-scatter.2.cloned.1.call-update) | async-done | bytes 131088 | tf_op jit(solution)/shard_map/reduce_scatter | solution.py:143
  155.9 2.5 %gather_fusion.5 = bf16[512,256]{1,0:T(8,128)(2,1)S(1)} fusion(bf16[256,256]{1,0:T(8,128)(2,1)} %bitcast.110, s32[1024]{0:T(1024)S(1)} %pad_clamp_fusion), kind=kCustom, calls=%fused_computation.5 | custom fusion | bytes 526336 | tf_op jit(solution)/shard_map/gather | solution.py:150
  158.4 0.8 select_convert_fusion
  159.2 4.6 %all-to-all-start.2 = ((bf16[4,2,64,256]{3,2,1,0:T(8,128)(2,1)}), bf16[4,2,64,256]{3,2,1,0:T(8,128)(2,1)S(1)}, u32[]{:S(2)}, u32[]{:S(2)}) async-start(bf16[4,2,64,256]{3,2,1,0:T(8,128)(2,1)} %select_convert_fusion), calls=%async_computation.3 | async-start | bytes 524288 | tf_op jit(solution)/shard_map/all_to_all | solution.py:152
  163.8 3.1 %convert_bitcast_fusion.1 = bf16[1,1024,1024]{2,1,0:T(8,128)(2,1)} fusion(bf16[128,1024]{1,0:T(8,128)(2,1)S(1)} %get-tuple-element.104, bf16[2,128,2048]{2,1,0:T(8,128)(2,1)} %all-gather.5.cloned.1.call-done, s32[]{:T(128)S(6)} %select_n.282, s32[]{:T(128)S(6)} %select_n.284), kind=kOutput, calls=%fused_computation.23 | convolution fusion | flops 269484032 | bytes 2621448 | tf_op jit(solution)/shard_map/dot_general | solution.py:124
  166.9 3.1 %convert_bitcast_fusion.2 = bf16[1,1024,1024]{2,1,0:T(8,128)(2,1)} fusion(bf16[128,1024]{1,0:T(8,128)(2,1)S(1)} %get-tuple-element.103, bf16[2,128,2048]{2,1,0:T(8,128)(2,1)} %all-gather.5.cloned.1.call-done, s32[]{:T(128)S(6)} %select_n.282, s32[]{:T(128)S(6)} %select_n.284), kind=kOutput, calls=%fused_computation.24 | convolution fusion | flops 269484032 | bytes 2621448 | tf_op jit(solution)/shard_map/dot_general | solution.py:121
  170.0 3.1 %convert_bitcast_fusion = bf16[1,1024,1024]{2,1,0:T(8,128)(2,1)} fusion(bf16[128,1024]{1,0:T(8,128)(2,1)S(1)} %get-tuple-element.99, f32[128]{0:T(128)S(1)} %fusion.46, bf16[2,128,2048]{2,1,0:T(8,128)(2,1)} %all-gather.3.cloned.1.call-done, s32[]{:T(128)S(6)} %select_n.282, s32[]{:T(128)S(6)} %select_n.284), kind=kOutput, calls=%fused_computation.22 | convolution fusion | flops 269877248 | bytes 2621960 | tf_op jit(solution)/shard_map/dot_general | solution.py:113
  173.1 3.8 %scatter_custom_fusion = f32[129,256]{1,0:T(8,128)S(1)} fusion(s32[512]{0:T(512)S(1)} %bitcast.122, bf16[512,256]{1,0:T(8,128)(2,1)S(1)} %bitcast.116, f32[]{:T(128)} %constant.168.clone.1), kind=kCustom, calls=%fused_computation.29 | custom fusion | flops 262144 | bytes 394244 | tf_op jit(solution)/shard_map/scatter-add | solution.py:159
  176.8 0.6 slice.34
  (109 shorter events, 2.6 us)
Async XLA Ops:
  7.2 66.7 %copy-start = (bf16[1,1024,1024]{2,1,0:T(8,128)(2,1)S(1)}, bf16[1,1024,1024]{2,1,0:T(8,128)(2,1)}, u32[]{:S(2)}) copy-start(bf16[1,1024,1024]{2,1,0:T(8,128)(2,1)} %param.11) | copy-start | bytes 6291460
  16.0 0.7 copy-start.1
  16.7 2.8 %copy-start.2 = (bf16[128,256]{1,0:T(8,128)(2,1)S(1)}, bf16[128,256]{1,0:T(8,128)(2,1)}, u32[]{:S(2)}) copy-start(bf16[128,256]{1,0:T(8,128)(2,1)} %param.9) | copy-start | bytes 196612
  19.2 2.2 %copy-start.3 = (bf16[128,256]{1,0:T(8,128)(2,1)S(1)}, bf16[128,256]{1,0:T(8,128)(2,1)}, u32[]{:S(2)}) copy-start(bf16[128,256]{1,0:T(8,128)(2,1)} %param.10) | copy-start | bytes 196612
  24.3 13.8 %all-to-all-start = ((bf16[4,2,64,256]{3,2,1,0:T(8,128)(2,1)}), bf16[4,2,64,256]{3,2,1,0:T(8,128)(2,1)S(1)}, u32[]{:S(2)}, u32[]{:S(2)}) async-start(bf16[4,2,64,256]{3,2,1,0:T(8,128)(2,1)} %get-tuple-element.107), calls=%async_computation | async-start | bytes 524288 | tf_op jit(solution)/shard_map/all_to_all | solution.py:56
  38.1 10.4 %all-to-all-start.1 = ((bf16[4,2,64,256]{3,2,1,0:T(8,128)(2,1)}), bf16[4,2,64,256]{3,2,1,0:T(8,128)(2,1)S(1)}, u32[]{:S(2)}, u32[]{:S(2)}) async-start(bf16[4,2,64,256]{3,2,1,0:T(8,128)(2,1)} %get-tuple-element.108), calls=%async_computation.1 | async-start | bytes 524288 | tf_op jit(solution)/shard_map/all_to_all | solution.py:55
  41.6 32.3 %all-gather.5.cloned.1.call-start = ((), (), s32[]{:S(2)}) async-start(), calls=%async_computation.5 | async-start | bytes 1179648 | tf_op jit(solution)/shard_map/all_gather | solution.py:76
  50.5 50.8 %all-gather.3.cloned.1.call-start = ((), (), s32[]{:S(2)}) async-start(), calls=%async_computation.4 | async-start | bytes 1179648 | tf_op jit(solution)/shard_map/all_gather | solution.py:77
  51.3 104.6 %reduce-scatter.2.cloned.1.call-start = ((), (), s32[]{:S(2)}) async-start(), calls=%async_computation.6 | async-start | bytes 1179648 | tf_op jit(solution)/shard_map/reduce_scatter | solution.py:143
  73.8 2.9 %copy-start.4 = (bf16[1,1024,1024]{2,1,0:T(8,128)(2,1)S(1)}, bf16[1,1024,1024]{2,1,0:T(8,128)(2,1)}, u32[]{:S(2)}) copy-start(bf16[1,1024,1024]{2,1,0:T(8,128)(2,1)} %param.12) | copy-start | bytes 6291460
  76.1 29.4 %collective-permute-start.2 = (bf16[128,1024]{1,0:T(8,128)(2,1)}, bf16[128,1024]{1,0:T(8,128)(2,1)S(1)}, u32[]{:S(2)}, u32[]{:S(2)}) collective-permute-start(bf16[128,1024]{1,0:T(8,128)(2,1)} %get-tuple-element.115), channel_id=1, source_target_pairs={{0,2},{2,0},{1,3},{3,1},{4,6},{6,4},{5,7},{7,5},{8,10},{10,8},{9,1... | collective-permute-start | bytes 786440 | tf_op jit(solution)/shard_map/ppermute | solution.py:14
  79.0 26.4 %copy-start.9 = (f32[2,128]{1,0:T(2,128)S(1)}, f32[2,128]{1,0:T(2,128)}, u32[]{:S(2)}) copy-start(f32[2,128]{1,0:T(2,128)} %param.14) | copy-start | bytes 3076
  79.0 26.5 %collective-permute-start.1 = (bf16[128,1024]{1,0:T(8,128)(2,1)}, bf16[128,1024]{1,0:T(8,128)(2,1)S(1)}, u32[]{:S(2)}, u32[]{:S(2)}) collective-permute-start(bf16[128,1024]{1,0:T(8,128)(2,1)} %get-tuple-element.113), channel_id=1, source_target_pairs={{0,2},{2,0},{1,3},{3,1},{4,6},{6,4},{5,7},{7,5},{8,10},{10,8},{9,1... | collective-permute-start | bytes 786440 | tf_op jit(solution)/shard_map/ppermute | solution.py:14
  104.7 8.7 %collective-permute-start = (bf16[128,1024]{1,0:T(8,128)(2,1)}, bf16[128,1024]{1,0:T(8,128)(2,1)S(1)}, u32[]{:S(2)}, u32[]{:S(2)}) collective-permute-start(bf16[128,1024]{1,0:T(8,128)(2,1)} %get-tuple-element.111), channel_id=1, source_target_pairs={{0,2},{2,0},{1,3},{3,1},{4,6},{6,4},{5,7},{7,5},{8,10},{10,8},{9,1... | collective-permute-start | bytes 786440 | tf_op jit(solution)/shard_map/ppermute | solution.py:14
  105.5 7.9 %copy-start.6 = (bf16[128,1024]{1,0:T(8,128)(2,1)}, bf16[128,1024]{1,0:T(8,128)(2,1)S(1)}, u32[]{:S(2)}) copy-start(bf16[128,1024]{1,0:T(8,128)(2,1)S(1)} %collective-permute-done.2) | copy-start | bytes 786436
  105.5 7.9 %copy-start.7 = (bf16[128,1024]{1,0:T(8,128)(2,1)}, bf16[128,1024]{1,0:T(8,128)(2,1)S(1)}, u32[]{:S(2)}) copy-start(bf16[128,1024]{1,0:T(8,128)(2,1)S(1)} %collective-permute-done.1) | copy-start | bytes 786436
  113.4 0.7 copy-start.8
  116.0 1.6 copy-start.5
  159.2 13.8 %all-to-all-start.2 = ((bf16[4,2,64,256]{3,2,1,0:T(8,128)(2,1)}), bf16[4,2,64,256]{3,2,1,0:T(8,128)(2,1)S(1)}, u32[]{:S(2)}, u32[]{:S(2)}) async-start(bf16[4,2,64,256]{3,2,1,0:T(8,128)(2,1)} %select_convert_fusion), calls=%async_computation.3 | async-start | bytes 524288 | tf_op jit(solution)/shard_map/all_to_all | solution.py:152
Sparse Core Ops, SparseCore 0:
  50.6 23.1 all-gather.4
  76.3 24.9 all-gather.2
  119.8 36.0 reduce-scatter.1
where the time goes:
time: 186 us; the launch traced here: 184 us
  waiting for transfers between devices  88.7 us (48%)
  local copies, waits for them, and re-layouts  24.5 us (13%)
  matrix products  19 us (10%)
  starting transfers between devices  15.6 us (8%)
  between operations  14.1 us (8%)
  other arithmetic  11.3 us (6%)
  blocking collectives  10.5 us (6%)
    reduce_scatter x1, waiting for transfers between devices, local(): lax.psum_scatter(padded, 'mp', scatter_dimension=1, tiled=True)  24.7 us
    all_gather x1, waiting for transfers between devices, local(): lax.all_gather(compact_in, 'mp', axis=2, tiled=True)  22.4 us
    all_gather x1, waiting for transfers between devices, local(): lax.all_gather(compact_out, 'mp', axis=2, tiled=True)  20.8 us
    psum x1, blocking collectives, local(): grad_combine = lax.psum(term_table, 'mp')  10.5 us
    ppermute x3, waiting for transfers between devices, from_partner(): return lax.ppermute(block, axis, route)  7.88 us
    gather x16, local copies, waits for them, and re-layouts, local(): jnp.searchsorted(row_keys, bounds, side='left')  6.69 us
    all_to_all x1, waiting for transfers between devices, local(): lax.all_to_all(send_out, 'expert', split_axis=0, concat_axis=0, tiled=True)  6.44 us
    all_to_all x1, waiting for transfers between devices, local(): lax.all_to_all(send_in, 'expert', split_axis=0, concat_axis=0, tiled=True)  5.7 us
  transfers between devices with their start and end apart: 9, of which 6 were waited for; matrix products, arithmetic and copies ran while one was open for 12% of the time, Pallas kernels for 0%

commit v1 on v0

v1 whole, which is shorter than its diff:
```python
import functools

import jax
import jax.numpy as jnp
from jax import lax
from jax.experimental import pallas as pl
from jax.experimental.pallas import tpu as pltpu
from jax.sharding import PartitionSpec as P

MESH = pl.DeviceIdType.MESH
F32 = jnp.float32
BF16 = jnp.bfloat16


def nn(a, b):
    return jnp.dot(a, b, preferred_element_type=F32)


def nt(a, b):
    return lax.dot_general(a, b, (((1,), (1,)), ((), ())), preferred_element_type=F32)


def tn(a, b):
    return lax.dot_general(a, b, (((0,), (0,)), ((), ())), preferred_element_type=F32)


def layer_kernel(
    dims,
    x_ref, cot_ref, wg_hbm, wu_hbm, wd_hbm, combine_ref, idx_ref,
    tokens_ref, terms_ref, rows_in_ref, scaled_ref, act_ref, dgate_ref, dup_ref,
    wg, wu, wd, tok, gathered, rx, rows_out, mine, ex_send, ex_recv,
    term_buf, red_send, red_recv, back_send, back_recv, ret_send, ret_recv,
    w_sem, z_send, z_recv, m_send, m_recv, f_send, x_send, x_recv,
    c_send, c_recv, r_send, r_recv, b_send, b_recv, t_send, t_recv,
):
    groups, lanes, exp_dev, blocks, half_lanes, tok_dev, width, capacity, hidden, chunk = dims
    chunks = hidden // chunk
    z = lax.axis_index("expert")
    lane = lax.axis_index("mp")
    own_b = lax.rem(lane, blocks)
    own_h = lax.rem(lax.div(lane, blocks), 2)
    own_e = lax.div(lane, 2 * blocks)
    feat_half = lax.div(lane, half_lanes)
    feat_pos = lax.rem(lane, half_lanes)

    def lane_of(e, h, b):
        return (e * 2 + h) * blocks + b

    def remote(src, dst, ssem, rsem, to_z, to_lane):
        return pltpu.make_async_remote_copy(
            src_ref=src, dst_ref=dst, send_sem=ssem, recv_sem=rsem,
            device_id=(to_z, to_lane), device_id_type=MESH,
        )

    def arrived(ref, ssem, rsem):
        remote(ref, ref, ssem, rsem, z, lane).wait_recv()

    loads = [
        pltpu.make_async_copy(src.at[0], dst, w_sem.at[i])
        for i, (src, dst) in enumerate(((wg_hbm, wg), (wu_hbm, wu), (wd_hbm, wd)))
    ]
    for load in loads:
        load.start()

    barrier = pltpu.get_barrier_semaphore()
    for d in range(1, groups):
        pl.semaphore_signal(barrier, inc=1, device_id=(lax.rem(z + d, groups), lane), device_id_type=MESH)
    for d in range(1, lanes):
        pl.semaphore_signal(barrier, inc=1, device_id=(z, lax.rem(lane + d, lanes)), device_id_type=MESH)
    pl.semaphore_wait(barrier, groups + lanes - 2)

    sends = []
    for kind, src in ((0, x_ref), (1, cot_ref)):
        for d in range(1, groups):
            copy = remote(src, tok.at[kind, z], z_send.at[kind, d], z_recv.at[kind, z],
                          lax.rem(z + d, groups), lane)
            copy.start()
            sends.append(copy)
    tok[0, z] = x_ref[...]
    tok[1, z] = cot_ref[...]

    eye = (
        lax.broadcasted_iota(jnp.int32, (capacity, capacity), 0)
        == lax.broadcasted_iota(jnp.int32, (capacity, capacity), 1)
    )

    def column(row):
        return jnp.sum(jnp.where(eye, jnp.broadcast_to(row, (capacity, capacity)), 0.0), axis=1, keepdims=True)

    idx_rows = [idx_ref[pl.ds(z * exp_dev + e, 1), :] for e in range(exp_dev)]
    idx_cols = [column(row.astype(F32)).astype(jnp.int32) for row in idx_rows]
    weight = column(combine_ref[pl.ds(own_e, 1), :])

    def exchange_rows(kind):
        for d in range(1, groups):
            s = lax.rem(z + d, groups)
            arrived(tok.at[kind, s], z_send.at[kind, d], z_recv.at[kind, s])
        for e in range(exp_dev):
            total = jnp.zeros((capacity, width), F32)
            for g in range(groups):
                ids = lax.broadcasted_iota(jnp.int32, (capacity, tok_dev), 1) + g * tok_dev
                pick = jnp.where(ids == idx_cols[e], 1.0, 0.0).astype(BF16)
                total += nn(pick, tok[kind, g])
            gathered[kind, e] = total.astype(BF16)
            target = lane_of(e, feat_half, own_b)

            @pl.when(target == lane)
            def _():
                rx[kind, feat_pos] = gathered[kind, e]

            @pl.when(target != lane)
            def _():
                remote(gathered.at[kind, e], rx.at[kind, feat_pos], m_send.at[kind, e],
                       m_recv.at[kind, feat_pos], z, target).start()

        for j in range(exp_dev):
            p = j * blocks + own_b
            source = own_h * half_lanes + p

            @pl.when(source != lane)
            def _():
                arrived(rx.at[kind, p], m_send.at[kind, 0], m_recv.at[kind, p])

            for d in range(1, blocks):
                copy = remote(rx.at[kind, p], rx.at[kind, p], f_send.at[kind, j, d], m_recv.at[kind, p],
                              z, lane_of(own_e, own_h, lax.rem(own_b + d, blocks)))
                copy.start()
                sends.append(copy)
        for d in range(1, blocks):
            for j in range(exp_dev):
                p = j * blocks + lax.rem(own_b + d, blocks)
                arrived(rx.at[kind, p], m_send.at[kind, 0], m_recv.at[kind, p])

    partner = lane_of(own_e, 1 - own_h, own_b)

    def exchange_sum(which, c, value):
        cols = slice(c * chunk, (c + 1) * chunk)
        mine[which, :, cols] = value
        ex_send[which, c] = value.astype(BF16)
        copy = remote(ex_send.at[which, c], ex_recv.at[which, c], x_send.at[which, c],
                      x_recv.at[which, c], z, partner)
        copy.start()
        sends.append(copy)

    exchange_rows(0)
    for p in range(half_lanes):
        rows_in_ref[:, p * width:(p + 1) * width] = rx[0, p]
    loads[0].wait()
    loads[1].wait()
    for c in range(chunks):
        cols = slice(c * chunk, (c + 1) * chunk)
        exchange_sum(0, c, nn(rows_in_ref[...], wg[:, cols]))
        exchange_sum(1, c, nn(rows_in_ref[...], wu[:, cols]))

    exchange_rows(1)
    for p in range(half_lanes):
        part = rx[1, p]
        rows_out[:, p * width:(p + 1) * width] = part
        scaled_ref[:, p * width:(p + 1) * width] = (weight * part.astype(F32)).astype(BF16)
    loads[2].wait()
    for c in range(chunks):
        cols = slice(c * chunk, (c + 1) * chunk)
        exchange_sum(2, c, nt(rows_out[...], wd[cols, :]))

    slot_term = jnp.zeros((capacity, 1), F32)
    for c in range(chunks):
        cols = slice(c * chunk, (c + 1) * chunk)
        for which in range(3):
            arrived(ex_recv.at[which, c], x_send.at[which, c], x_recv.at[which, c])
        gate = mine[0, :, cols] + ex_recv[0, c].astype(F32)
        up = mine[1, :, cols] + ex_recv[1, c].astype(F32)
        back = mine[2, :, cols] + ex_recv[2, c].astype(F32)
        s = jax.nn.sigmoid(gate)
        act = (gate * s * up).astype(BF16)
        act_ref[:, cols] = act
        slot_term += jnp.sum(act.astype(F32) * back, axis=1, keepdims=True)
        a = weight * back
        dgate_ref[:, cols] = (a * up * s * (1.0 + gate * (1.0 - s))).astype(BF16)
        dup_ref[:, cols] = (a * gate * s).astype(BF16)

    def block_part(p):
        rows = pl.ds(pl.multiple_of(p * width, width), width)
        return nt(dgate_ref[...], wg[rows, :]) + nt(dup_ref[...], wu[rows, :])

    for d in range(1, blocks):
        to_b = lax.rem(own_b + d, blocks)
        for j in range(exp_dev):
            red_send[d, j] = block_part(j * blocks + to_b).astype(BF16)
            copy = remote(red_send.at[d, j], red_recv.at[own_b, j], r_send.at[d, j], r_recv.at[own_b, j],
                          z, lane_of(own_e, own_h, to_b))
            copy.start()
            sends.append(copy)
    for j in range(exp_dev):
        total = block_part(j * blocks + own_b).astype(BF16).astype(F32)
        for d in range(1, blocks):
            from_b = lax.rem(own_b + d, blocks)
            arrived(red_recv.at[from_b, j], r_send.at[d, j], r_recv.at[from_b, j])
            total += red_recv[from_b, j].astype(F32)
        back_send[j] = total.astype(BF16)
        target = own_h * half_lanes + j * blocks + own_b

        @pl.when(target == lane)
        def _():
            back_recv[own_e] = back_send[j]

        @pl.when(target != lane)
        def _():
            remote(back_send.at[j], back_recv.at[own_e], b_send.at[j], b_recv.at[own_e], z, target).start()

    term_row = jnp.sum(jnp.where(eye, jnp.broadcast_to(slot_term, (capacity, capacity)), 0.0), axis=0, keepdims=True)

    @pl.when(own_h == 0)
    def _():
        term_buf[own_e, own_b] = jnp.broadcast_to(term_row, (8, capacity))
        for d in range(1, lanes):
            remote(term_buf.at[own_e, own_b], term_buf.at[own_e, own_b], c_send.at[d],
                   c_recv.at[own_e, own_b], z, lax.rem(lane + d, lanes)).start()

    for e in range(exp_dev):
        source = lane_of(e, feat_half, own_b)

        @pl.when(source != lane)
        def _():
            arrived(back_recv.at[e], b_send.at[0], b_recv.at[e])

    def token_part(g):
        total = jnp.zeros((tok_dev, width), F32)
        for e in range(exp_dev):
            ids = lax.broadcasted_iota(jnp.int32, (tok_dev, capacity), 0) + g * tok_dev
            put = jnp.where(ids == idx_rows[e], 1.0, 0.0).astype(BF16)
            total += nn(put, back_recv[e])
        return total

    for d in range(1, groups):
        g = lax.rem(z + d, groups)
        ret_send[d] = token_part(g).astype(BF16)
        copy = remote(ret_send.at[d], ret_recv.at[z], t_send.at[d], t_recv.at[z], g, lane)
        copy.start()
        sends.append(copy)
    total = token_part(z)

    for e in range(exp_dev):
        for b in range(blocks):
            @pl.when(lane_of(e, 0, b) != lane)
            def _():
                arrived(term_buf.at[e, b], c_send.at[1], c_recv.at[e, b])
        row = term_buf[e, 0, 0:1, :]
        for b in range(1, blocks):
            row += term_buf[e, b, 0:1, :]
        terms_ref[e:e + 1, :] = row

    for d in range(1, groups):
        g = lax.rem(z + d, groups)
        arrived(ret_recv.at[g], t_send.at[d], t_recv.at[g])
        total += ret_recv[g].astype(F32)
    tokens_ref[...] = total.astype(BF16)

    for copy in sends:
        copy.wait_send()
    for e in range(exp_dev):
        target = lane_of(e, feat_half, own_b)

        @pl.when(target != lane)
        def _():
            for kind in range(2):
                remote(gathered.at[kind, e], rx.at[kind, feat_pos], m_send.at[kind, e],
                       m_recv.at[kind, feat_pos], z, target).wait_send()

    for j in range(exp_dev):
        target = own_h * half_lanes + j * blocks + own_b

        @pl.when(target != lane)
        def _():
            remote(back_send.at[j], back_recv.at[own_e], b_send.at[j], b_recv.at[own_e], z, target).wait_send()

    @pl.when(own_h == 0)
    def _():
        for d in range(1, lanes):
            remote(term_buf.at[own_e, own_b], term_buf.at[own_e, own_b], c_send.at[d],
                   c_recv.at[own_e, own_b], z, lax.rem(lane + d, lanes)).wait_send()


def weight_kernel(rows_in, scaled, act, dgate, dup, out_gate, out_up, out_down):
    out_gate[0] = tn(rows_in[...], dgate[...]).astype(BF16)
    out_up[0] = tn(rows_in[...], dup[...]).astype(BF16)
    out_down[0] = tn(act[...], scaled[...]).astype(BF16)


def local(x_tokens, cotangent, w_gate, w_up, w_down, combine, indices):
    groups = lax.axis_size("expert")
    lanes = lax.axis_size("mp")
    tok_dev, width = x_tokens.shape
    experts, capacity = indices.shape
    exp_dev = experts // groups
    blocks = lanes // (2 * exp_dev)
    half_lanes = lanes // 2
    half_width, hidden = w_gate.shape[1:]
    chunk = min(hidden, 256)
    chunks = hidden // chunk
    dims = (groups, lanes, exp_dev, blocks, half_lanes, tok_dev, width, capacity, hidden, chunk)
    vmem = pl.BlockSpec(memory_space=pltpu.VMEM)
    anywhere = pl.BlockSpec(memory_space=pl.ANY)
    dma = pltpu.SemaphoreType.DMA
    slot_half = jax.ShapeDtypeStruct((capacity, half_width), BF16)
    slot_hidden = jax.ShapeDtypeStruct((capacity, hidden), BF16)
    grad_tokens, grad_combine, rows_in, scaled, act, dgate, dup = pl.pallas_call(
        functools.partial(layer_kernel, dims),
        out_shape=[
            jax.ShapeDtypeStruct((tok_dev, width), BF16),
            jax.ShapeDtypeStruct((exp_dev, capacity), F32),
            slot_half, slot_half, slot_hidden, slot_hidden, slot_hidden,
        ],
        in_specs=[vmem, vmem, anywhere, anywhere, anywhere, vmem, vmem],
        out_specs=[vmem] * 7,
        scratch_shapes=[
            pltpu.VMEM((half_width, hidden), BF16),
            pltpu.VMEM((half_width, hidden), BF16),
            pltpu.VMEM((hidden, half_width), BF16),
            pltpu.VMEM((2, groups, tok_dev, width), BF16),
            pltpu.VMEM((2, exp_dev, capacity, width), BF16),
            pltpu.VMEM((2, half_lanes, capacity, width), BF16),
            pltpu.VMEM((capacity, half_width), BF16),
            pltpu.VMEM((3, capacity, hidden), F32),
            pltpu.VMEM((3, chunks, capacity, chunk), BF16),
            pltpu.VMEM((3, chunks, capacity, chunk), BF16),
            pltpu.VMEM((exp_dev, blocks, 8, capacity), F32),
            pltpu.VMEM((blocks, exp_dev, capacity, width), BF16),
            pltpu.VMEM((blocks, exp_dev, capacity, width), BF16),
            pltpu.VMEM((exp_dev, capacity, width), BF16),
            pltpu.VMEM((exp_dev, capacity, width), BF16),
            pltpu.VMEM((groups, tok_dev, width), BF16),
            pltpu.VMEM((groups, tok_dev, width), BF16),
            dma((3,)), dma((2, groups)), dma((2, groups)),
            dma((2, exp_dev)), dma((2, half_lanes)), dma((2, exp_dev, blocks)),
            dma((3, chunks)), dma((3, chunks)),
            dma((lanes,)), dma((exp_dev, blocks)),
            dma((blocks, exp_dev)), dma((blocks, exp_dev)),
            dma((exp_dev,)), dma((exp_dev,)),
            dma((groups,)), dma((groups,)),
        ],
        compiler_params=pltpu.CompilerParams(
            collective_id=0, has_side_effects=True, vmem_limit_bytes=40 * 1024 * 1024
        ),
        name="layer",
    )(x_tokens, cotangent, w_gate, w_up, w_down, combine, indices)

    steps = min(4, hidden // 128)
    rows = half_width // steps
    units = hidden // steps
    grad_gate, grad_up, grad_down = pl.pallas_call(
        weight_kernel,
        grid=(steps,),
        out_shape=[
            jax.ShapeDtypeStruct(w_gate.shape, BF16),
            jax.ShapeDtypeStruct(w_up.shape, BF16),
            jax.ShapeDtypeStruct(w_down.shape, BF16),
        ],
        in_specs=[
            pl.BlockSpec((capacity, rows), lambda i: (0, i)),
            pl.BlockSpec((capacity, half_width), lambda i: (0, 0)),
            pl.BlockSpec((capacity, units), lambda i: (0, i)),
            pl.BlockSpec((capacity, hidden), lambda i: (0, 0)),
            pl.BlockSpec((capacity, hidden), lambda i: (0, 0)),
        ],
        out_specs=[
            pl.BlockSpec((1, rows, hidden), lambda i: (0, i, 0)),
            pl.BlockSpec((1, rows, hidden), lambda i: (0, i, 0)),
            pl.BlockSpec((1, units, half_width), lambda i: (0, i, 0)),
        ],
        compiler_params=pltpu.CompilerParams(vmem_limit_bytes=32 * 1024 * 1024),
        name="weight_grads",
    )(rows_in, scaled, act, dgate, dup)
    return grad_tokens, grad_gate, grad_up, grad_down, grad_combine


def solution(mesh):
    placed = (
        P("expert", "mp"),
        P("expert", "mp"),
        P("expert", None, "mp"),
        P("expert", None, "mp"),
        P("expert", "mp", None),
        P("expert", None),
        P(),
    )
    return jax.shard_map(
        local,
        mesh=mesh,
        in_specs=placed,
        out_specs=(
            P("expert", "mp"),
            P("expert", None, "mp"),
            P("expert", None, "mp"),
            P("expert", "mp", None),
            P("expert", None),
        ),
        check_vma=False,
    )
```

time: 186 us -> 72.6 us (0.39)
  waiting for transfers between devices: 88.7 us -> 0 us
  Pallas kernels: 0 us -> 61.5 us
  matrix products: 19 us -> 0 us
  starting transfers between devices: 15.6 us -> 0 us
  local copies, waits for them, and re-layouts: 24.5 us -> 9 us
  between operations: 14.1 us -> 0.66 us
  other arithmetic: 11.3 us -> 0 us
  blocking collectives: 10.5 us -> 0 us
    pallas_call x0 -> x2, Pallas kernels: none -> 61.5 us  [the longest x1 57.6 us: local(): pl.pallas_call(functools.partial(layer_kernel, dims), out_shape=[jax.Shap...]
    all_gather x2 -> x0, waiting for transfers between devices: 43.2 us -> none  [the longest x1 22.4 us: local(): lax.all_gather(compact_in, 'mp', axis=2, tiled=True)]
    reduce_scatter x1 -> x0, waiting for transfers between devices: 24.7 us -> none  [local(): lax.psum_scatter(padded, 'mp', scatter_dimension=1, tiled=True)]
    gather x25 -> x0, local copies, waits for them, and re-layouts: 20.4 us -> none  [the longest x16 6.69 us: local(): jnp.searchsorted(row_keys, bounds, side='left')]
    dot_general x8 -> x0, matrix products: 19 us -> none  [the longest x1 3.4 us: local(): lax.dot_general(rows_out, wd, (((1,), (1,)), ((), ())), preferred_element...]
    all_to_all x3 -> x0, starting transfers between devices: 12.9 us -> none  [the longest x1 4.87 us: local(): lax.all_to_all(send_out, 'expert', split_axis=0, concat_axis=0, tiled=True)]
    all_to_all x3 -> x0, waiting for transfers between devices: 12.1 us -> none  [the longest x1 6.44 us: local(): lax.all_to_all(send_out, 'expert', split_axis=0, concat_axis=0, tiled=True)]
    psum x1 -> x0, blocking collectives: 10.5 us -> none  [local(): grad_combine = lax.psum(term_table, 'mp')]
  transfers between devices with their start and end apart: 9 -> 0, of which waited for: 6 -> 0; matrix products, arithmetic and copies ran while one was open for 12% -> 0% of each run, Pallas kernels for 0% -> 0%
where the time goes in v1:
time: 72.6 us; the launch traced here: 71.2 us
  Pallas kernels  61.5 us (85%)
  local copies, waits for them, and re-layouts  9 us (12%)
    pallas_call x1, Pallas kernels, local(): pl.pallas_call(functools.partial(layer_kernel, dims), out_shape=[jax.Shap...  57.6 us
    unnamed x16, local copies, waits for them, and re-layouts  9 us
    pallas_call x1, Pallas kernels, local(): pl.pallas_call(weight_kernel, grid=(steps,), out_shape=[jax.ShapeDtypeStr...  3.88 us

profile of v1, /device:TPU:2, one launch (start us, length us, event | category | flops | bytes accessed | tf_op | source)
XLA Modules:
  0.0 71.2 jit_solution(12308983376516023194)
XLA Ops:
  0.6 0.0 copy-start
  0.6 1.6 %copy-done = bf16[1,1024,1024]{2,1,0:T(8,128)(2,1)S(1)} copy-done((bf16[1,1024,1024]{2,1,0:T(8,128)(2,1)S(1)}, bf16[1,1024,1024]{2,1,0:T(8,128)(2,1)}, u32[]{:S(2)}) %copy-start) | copy-done | bytes 2097176
  2.2 0.0 copy-start.1
  2.2 1.6 %copy-done.1 = bf16[1,1024,1024]{2,1,0:T(8,128)(2,1)S(1)} copy-done((bf16[1,1024,1024]{2,1,0:T(8,128)(2,1)S(1)}, bf16[1,1024,1024]{2,1,0:T(8,128)(2,1)}, u32[]{:S(2)}) %copy-start.1) | copy-done | bytes 2097176
  3.8 0.0 copy-start.2
  3.8 1.6 %copy-done.2 = bf16[1,1024,1024]{2,1,0:T(8,128)(2,1)S(1)} copy-done((bf16[1,1024,1024]{2,1,0:T(8,128)(2,1)S(1)}, bf16[1,1024,1024]{2,1,0:T(8,128)(2,1)}, u32[]{:S(2)}) %copy-start.2) | copy-done | bytes 2097176
  5.4 0.0 copy-start.3
  5.4 0.8 %copy-done.3 = bf16[128,256]{1,0:T(8,128)(2,1)S(1)} copy-done((bf16[128,256]{1,0:T(8,128)(2,1)S(1)}, bf16[128,256]{1,0:T(8,128)(2,1)}, u32[]{:S(2)}) %copy-start.3) | copy-done | bytes 65560
  6.2 0.0 copy-start.4
  6.3 0.8 %copy-done.4 = bf16[128,256]{1,0:T(8,128)(2,1)S(1)} copy-done((bf16[128,256]{1,0:T(8,128)(2,1)S(1)}, bf16[128,256]{1,0:T(8,128)(2,1)}, u32[]{:S(2)}) %copy-start.4) | copy-done | bytes 65560
  7.1 0.0 copy-start.5
  7.1 0.7 copy-done.5
  7.8 0.0 copy-start.6
  7.8 0.7 copy-done.6
  8.5 57.6 %layer.1 = (bf16[128,256]{1,0:T(8,128)(2,1)S(1)}, f32[2,128]{1,0:T(2,128)S(1)}, bf16[128,1024]{1,0:T(8,128)(2,1)S(1)}, bf16[128,1024]{1,0:T(8,128)(2,1)S(1)}, bf...) custom-call(bf16[128,256]{1,0:T(8,128)(2,1)S(1)} %copy-done.3, ...), custom_call_target="tpu_custom_call" | custom-call | tf_op jit(solution)/shard_map/layer/pallas_call | solution.py:306
  66.1 3.9 %weight_grads.1 = (bf16[1,1024,1024]{2,1,0:T(8,128)(2,1)}, bf16[1,1024,1024]{2,1,0:T(8,128)(2,1)}, bf16[1,1024,1024]{2,1,0:T(8,128)(2,1)}) custom-call(bf16[128,1024]{1,0:T(8,128)(2,1)S(1)} %get-tuple-element.16.rows_in, bf16[128,1024]{1,0:T(8,128)(2,1)S(1)} %get-tuple-element.17.scaled, bf16[128,1024]{1,0:T(8,128)(2,1)S(1)} %get-tuple-element.18.act, ...), custom_call_target="tpu_custom_call" | custom-call | tf_op jit(solution)/shard_map/weight_grads/pallas_call | solution.py:350
  70.0 0.6 copy.14
  70.6 0.6 copy.15
Async XLA Ops:
  0.6 1.6 %copy-start = (bf16[1,1024,1024]{2,1,0:T(8,128)(2,1)S(1)}, bf16[1,1024,1024]{2,1,0:T(8,128)(2,1)}, u32[]{:S(2)}) copy-start(bf16[1,1024,1024]{2,1,0:T(8,128)(2,1)} %wg_hbm.1) | copy-start | bytes 6291460
  2.2 1.6 %copy-start.1 = (bf16[1,1024,1024]{2,1,0:T(8,128)(2,1)S(1)}, bf16[1,1024,1024]{2,1,0:T(8,128)(2,1)}, u32[]{:S(2)}) copy-start(bf16[1,1024,1024]{2,1,0:T(8,128)(2,1)} %wu_hbm.1) | copy-start | bytes 6291460
  3.8 1.6 %copy-start.2 = (bf16[1,1024,1024]{2,1,0:T(8,128)(2,1)S(1)}, bf16[1,1024,1024]{2,1,0:T(8,128)(2,1)}, u32[]{:S(2)}) copy-start(bf16[1,1024,1024]{2,1,0:T(8,128)(2,1)} %wd_hbm.1) | copy-start | bytes 6291460
  5.4 0.8 %copy-start.3 = (bf16[128,256]{1,0:T(8,128)(2,1)S(1)}, bf16[128,256]{1,0:T(8,128)(2,1)}, u32[]{:S(2)}) copy-start(bf16[128,256]{1,0:T(8,128)(2,1)} %x_ref.1) | copy-start | bytes 196612
  6.2 0.8 %copy-start.4 = (bf16[128,256]{1,0:T(8,128)(2,1)S(1)}, bf16[128,256]{1,0:T(8,128)(2,1)}, u32[]{:S(2)}) copy-start(bf16[128,256]{1,0:T(8,128)(2,1)} %cot_ref.1) | copy-start | bytes 196612
  7.1 0.7 copy-start.5
  7.8 0.7 copy-start.6
